TPU v7x, 128 devices: a whole 4x4x4 slice. The times are simulated.
128 devices in a mesh: dp: 32 (over z, x, core), proto: 4 (over y).
Axes of the slice: x: 4, y: 4, z: 4, core: 2. Of those that a mesh axis runs over, the one named last changes fastest.
Arguments:
- teacher_feats: bfloat16 [8192, 256], P('dp'), may hold values from -10 to 10
- teacher_protos: bfloat16 [256, 65536], P(None, 'proto'), may hold values from -1 to 1
- student_feats: bfloat16 [8192, 256], P('dp'), may hold values from -10 to 10
- student_protos: bfloat16 [256, 65536], P(None, 'proto'), may hold values from -1 to 1
Outputs:
- grad_protos: float32 [256, 65536], P('dp', 'proto')
- grad_feats: float32 [8192, 256], P('dp')
All inputs are finite; a program needn't handle non-finite values.
Results may differ from a plain program's by a relative error of at most 0.0028.
Values may be sent and summed in bfloat16 or wider, within the bound.
A program may use at most 192 MiB of HBM per device.

v0:
```python
import math

import jax
import jax.numpy as jnp
from jax import lax
from jax.sharding import PartitionSpec as P

ITERS = 3


TEACHER_TEMP = 0.04
STUDENT_TEMP = 0.1


def per_device(teacher_feats, teacher_protos, student_feats, student_protos):
    img_rows, feat_width = student_feats.shape
    local_protos = teacher_protos.shape[1]
    data_size = lax.axis_size("dp")
    proto_size = lax.axis_size("proto")
    images = img_rows * data_size
    protos = local_protos * proto_size
    scores = (
        jnp.dot(teacher_feats, teacher_protos, preferred_element_type=jnp.float32) / TEACHER_TEMP
    )
    col_max = lax.pmax(jnp.max(scores, axis=0).astype(jnp.bfloat16), "dp").astype(jnp.float32)
    exp_table = jnp.exp(scores - col_max[None, :])
    col_total = lax.psum(jnp.sum(exp_table, axis=0), "dp")
    col_scale = 1.0 / col_total
    row_scale = jnp.ones((img_rows,), jnp.float32)
    for iteration in range(ITERS):
        if iteration > 0:
            col_scale = 1.0 / lax.psum(jnp.sum(exp_table * row_scale[:, None], axis=0), "dp")
        row_scale = 1.0 / lax.psum(jnp.sum(exp_table * col_scale[None, :], axis=1), "proto")
    student_scores = (
        jnp.dot(student_feats, student_protos, preferred_element_type=jnp.float32) / STUDENT_TEMP
    )
    row_top = lax.pmax(jnp.max(student_scores, axis=1), "proto")
    exp_rows = jnp.exp(student_scores - row_top[:, None])
    row_total = lax.psum(jnp.sum(exp_rows, axis=1), "proto")
    probabilities = exp_rows / row_total[:, None]
    targets = exp_table * col_scale[None, :] * row_scale[:, None]
    grad_logits = ((probabilities - targets) * (protos / STUDENT_TEMP)).astype(jnp.bfloat16)
    partial_grad = lax.dot_general(
        grad_logits, student_protos, (((1,), (1,)), ((), ())), preferred_element_type=jnp.float32
    )
    grad_feats = lax.psum(partial_grad, "proto") / math.sqrt(protos)
    summed = lax.psum_scatter(
        lax.dot_general(
            student_feats, grad_logits, (((0,), (0,)), ((), ())), preferred_element_type=jnp.float32
        ),
        "dp",
        scatter_dimension=0,
        tiled=True,
    )
    grad_protos = summed / math.sqrt(images)
    return (grad_protos, grad_feats)


def solution(mesh):
    return jax.shard_map(
        per_device,
        mesh=mesh,
        in_specs=(P("dp", None), P(None, "proto"), P("dp", None), P(None, "proto")),
        out_specs=(P("dp", "proto"), P("dp", None)),
        check_vma=False,
    )
```

profile of v0, /device:TPU:1, one launch (start us, length us, event | category | flops | bytes accessed | tf_op | source)
XLA Modules:
  0.0 716.7 jit_solution(8662130624413247193)
XLA Ops:
  7.2 11.6 %fusion.2 = (bf16[16384]{0:T(1024)(128)(2,1)S(1)}, f32[256,16384]{1,0:T(8,128)}) fusion(bf16[256,256]{1,0:T(8,128)(2,1)} %param.4, bf16[256,16384]{1,0:T(8,128)(2,1)} %param.5), kind=kOutput, calls=%fused_computation.21 | convolution fusion | flops 2155855872 | bytes 25329664 | tf_op jit(solution)/shard_map/dot_general | solution.py:23
  18.8 125.3 %pmax.15 = bf16[16384]{0:T(1024)(128)(2,1)S(1)} all-reduce(bf16[16384]{0:T(1024)(128)(2,1)S(1)} %get-tuple-element.8), channel_id=1, replica_groups=mesh['dp'=32,'proto'=4] {'dp'}, use_global_device_ids=true, to_apply=%region_5.0 | all-reduce | flops 16384 | bytes 65536 | tf_op jit(solution)/shard_map/pmax | solution.py:25
  144.1 8.9 %fusion.1 = f32[16384]{0:T(1024)} fusion(f32[256,16384]{1,0:T(8,128)} %get-tuple-element.9, f32[16384]{0:T(1024)S(1)} %convert_element_type.10), kind=kLoop, calls=%fused_computation.12 | loop fusion | flops 8372224 | bytes 16908288 | tf_op jit(solution)/shard_map/reduce_sum | solution.py:27
  153.1 97.2 %all-reduce.6.cloned.1.call-done = f32[16384]{0:T(1024)} async-done(((f32[16384]{0:T(1024)}), f32[16384]{0:T(1024)}) %all-reduce.6.cloned.1.call-update) | async-done | bytes 65552 | tf_op jit(solution)/shard_map/psum | solution.py:27
  250.3 0.9 broadcast_divide_fusion.2
  251.2 8.9 %multiply_reduce_fusion.3 = f32[256]{0:T(256)S(1)} fusion(f32[16384]{0:T(1024)S(1)} %broadcast_divide_fusion.2, f32[256,16384]{1,0:T(8,128)} %get-tuple-element.9, f32[16384]{0:T(1024)S(1)} %convert_element_type.10), kind=kLoop, calls=%fused_computation.7 | loop fusion | flops 12582656 | bytes 16909312 | tf_op jit(solution)/shard_map/reduce_sum | solution.py:33
  260.1 8.5 %psum.58 = f32[256]{0:T(256)S(1)} all-reduce(f32[256]{0:T(256)S(1)} %multiply_reduce_fusion.3), channel_id=1, replica_groups=mesh['dp'=32,'proto'=4] {'proto'}, use_global_device_ids=true, to_apply=%region_9.0 | all-reduce | flops 256 | bytes 2048 | tf_op jit(solution)/shard_map/psum | solution.py:33
  268.6 9.3 %multiply_reduce_fusion.2 = f32[16384]{0:T(1024)} fusion(f32[256]{0:T(256)S(1)} %broadcast_divide_fusion.5, f32[256,16384]{1,0:T(8,128)} %get-tuple-element.9, f32[16384]{0:T(1024)S(1)} %convert_element_type.10), kind=kLoop, calls=%fused_computation.6 | loop fusion | flops 12566528 | bytes 16909312 | tf_op jit(solution)/shard_map/reduce_sum | solution.py:32
  278.1 11.5 %fusion.3 = (f32[256]{0:T(256)S(1)}, f32[256,16384]{1,0:T(8,128)}) fusion(bf16[256,256]{1,0:T(8,128)(2,1)S(1)} %copy-done, bf16[256,16384]{1,0:T(8,128)(2,1)} %param.7), kind=kOutput, calls=%fused_computation.22 | convolution fusion | flops 2155872000 | bytes 25297920 | tf_op jit(solution)/shard_map/dot_general | solution.py:35
  289.6 6.0 pmax.14
  295.6 76.5 %all-reduce.8.cloned.1.call-done = f32[16384]{0:T(1024)} async-done(((f32[16384]{0:T(1024)}), f32[16384]{0:T(1024)}) %all-reduce.8.cloned.1.call-update) | async-done | bytes 65552 | tf_op jit(solution)/shard_map/psum | solution.py:32
  372.1 0.9 broadcast_divide_fusion.1
  373.0 8.9 %multiply_reduce_fusion.1 = f32[256]{0:T(256)S(1)} fusion(f32[16384]{0:T(1024)S(1)} %broadcast_divide_fusion.1, f32[256,16384]{1,0:T(8,128)} %get-tuple-element.9, f32[16384]{0:T(1024)S(1)} %convert_element_type.10), kind=kLoop, calls=%fused_computation.5 | loop fusion | flops 12582656 | bytes 16909312 | tf_op jit(solution)/shard_map/reduce_sum | solution.py:33
  381.9 8.5 %psum.60 = f32[256]{0:T(256)S(1)} all-reduce(f32[256]{0:T(256)S(1)} %multiply_reduce_fusion.1), channel_id=1, replica_groups=mesh['dp'=32,'proto'=4] {'proto'}, use_global_device_ids=true, to_apply=%region_13.0 | all-reduce | flops 256 | bytes 2048 | tf_op jit(solution)/shard_map/psum | solution.py:33
  390.4 9.3 %multiply_reduce_fusion = f32[16384]{0:T(1024)} fusion(f32[256]{0:T(256)S(1)} %broadcast_divide_fusion.4, f32[256,16384]{1,0:T(8,128)} %get-tuple-element.9, f32[16384]{0:T(1024)S(1)} %convert_element_type.10), kind=kLoop, calls=%fused_computation.4 | loop fusion | flops 12566528 | bytes 16909312 | tf_op jit(solution)/shard_map/reduce_sum | solution.py:32
  399.9 8.1 %fusion = f32[256]{0:T(256)S(1)} fusion(f32[256,16384]{1,0:T(8,128)} %get-tuple-element.11, f32[256]{0:T(256)S(1)} %pmax.14), kind=kLoop, calls=%fused_computation.11 | loop fusion | flops 8388352 | bytes 16779264 | tf_op jit(solution)/shard_map/reduce_sum | solution.py:39
  408.1 85.8 %all-reduce.10.cloned.1.call-done = f32[16384]{0:T(1024)} async-done(((f32[16384]{0:T(1024)}), f32[16384]{0:T(1024)}) %all-reduce.10.cloned.1.call-update) | async-done | bytes 65552 | tf_op jit(solution)/shard_map/psum | solution.py:32
  493.9 0.9 broadcast_divide_fusion
  494.7 8.6 %multiply_reduce_fusion.4 = f32[256]{0:T(256)S(1)} fusion(f32[16384]{0:T(1024)S(1)} %broadcast_divide_fusion, f32[256,16384]{1,0:T(8,128)} %get-tuple-element.9, f32[16384]{0:T(1024)S(1)} %convert_element_type.10), kind=kLoop, calls=%fused_computation.10 | loop fusion | flops 12582656 | bytes 16909312 | tf_op jit(solution)/shard_map/reduce_sum | solution.py:33
  503.4 8.5 %all-reduce = (f32[256]{0:T(256)S(1)}, f32[256]{0:T(256)S(1)}) all-reduce(f32[256]{0:T(256)S(1)} %multiply_reduce_fusion.4, f32[256]{0:T(256)S(1)} %fusion), channel_id=1, replica_groups=mesh['dp'=32,'proto'=4] {'proto'}, use_global_device_ids=true, to_apply=%region_17.0 | all-reduce | flops 512 | bytes 4096 | tf_op jit(solution)/shard_map/psum | solution.py:33
  511.8 12.7 %multiply_convert_fusion = bf16[256,16384]{1,0:T(8,128)(2,1)S(1)} fusion(f32[256,16384]{1,0:T(8,128)} %get-tuple-element.11, f32[256]{0:T(256)S(1)} %broadcast_divide_fusion.3, f32[16384]{0:T(1024)S(1)} %broadcast_divide_fusion, f32[256]{0:T(256)S(1)} %get-tuple-element.7, f32[256]{0:T(256)S(1)} %pmax.14, f32[256,16384]{1,0:T(8,128)} %get-tuple-element.9, ...), kind=kLoop, calls=%fused_computation.3 | loop fusion | flops 33554432 | bytes 42077184 | tf_op jit(solution)/shard_map/convert_element_type | solution.py:42
  524.6 3.2 copy-done.1
  527.8 6.4 fusion.4
  534.3 0.3 reduce-scatter.4.cloned.1.call-start
  534.6 11.5 %convolution_bitcast_fusion = f32[256,16384]{0,1:T(8,128)} fusion(bf16[256,16384]{1,0:T(8,128)(2,1)} %copy-done.1, bf16[256,256]{1,0:T(8,128)(2,1)S(1)} %copy-done), kind=kOutput, calls=%fused_computation | convolution fusion | flops 2147483648 | bytes 25296896 | tf_op jit(solution)/shard_map/dot_general | solution.py:48
  546.1 17.4 %copy.8 = f32[256,16384]{1,0:T(8,128)} copy(f32[256,16384]{0,1:T(8,128)} %convolution_bitcast_fusion) | data formatting | bytes 33554432
  563.6 8.8 %all-reduce.12.cloned.1.call-done = f32[256,256]{1,0:T(8,128)} async-done(((f32[256,256]{1,0:T(8,128)}), f32[256,256]{1,0:T(8,128)}) %all-reduce.12.cloned.1.call-update) | async-done | bytes 262160 | tf_op jit(solution)/shard_map/psum | solution.py:46
  572.4 1.7 broadcast_multiply_fusion.1
  574.0 118.8 %reduce-scatter.4.cloned.1.call-done = f32[8,16384]{1,0:T(8,128)} async-done(((f32[256,16384]{1,0:T(8,128)}), f32[8,16384]{1,0:T(8,128)}) %reduce-scatter.4.cloned.1.call-update) | async-done | bytes 524304
  692.8 5.7 copy.9
  698.5 5.8 broadcast_multiply_fusion
  704.3 5.9 copy.7
  (16 shorter events, 0.7 us)
Async XLA Ops:
  7.2 270.9 %copy-start = (bf16[256,256]{1,0:T(8,128)(2,1)S(1)}, bf16[256,256]{1,0:T(8,128)(2,1)}, u32[]{:S(2)}) copy-start(bf16[256,256]{1,0:T(8,128)(2,1)} %param.6) | copy-start | bytes 393220
  7.2 243.2 %all-reduce.6.cloned.1.call-start = ((), (), s32[]{:S(2)}) async-start(), calls=%async_computation.1 | async-start | bytes 131072 | tf_op jit(solution)/shard_map/psum | solution.py:27
  153.1 219.1 %all-reduce.8.cloned.1.call-start = ((), (), s32[]{:S(2)}) async-start(), calls=%async_computation.2 | async-start | bytes 131072 | tf_op jit(solution)/shard_map/psum | solution.py:32
  277.9 216.0 %all-reduce.10.cloned.1.call-start = ((), (), s32[]{:S(2)}) async-start(), calls=%async_computation.3 | async-start | bytes 131072 | tf_op jit(solution)/shard_map/psum | solution.py:32
  399.7 172.7 %all-reduce.12.cloned.1.call-start = ((), (), s32[]{:S(2)}) async-start(), calls=%async_computation.4 | async-start | bytes 524288 | tf_op jit(solution)/shard_map/psum | solution.py:46
  524.6 3.2 copy-start.1
  534.3 158.6 %reduce-scatter.4.cloned.1.call-start = ((), (), s32[]{:S(2)}) async-start(), calls=%async_computation.5 | async-start | bytes 17301504
Sparse Core Ops, SparseCore 0:
  153.2 97.1 all-reduce.5
  278.0 94.0 all-reduce.7
  399.8 94.0 all-reduce.9
  534.4 37.9 all-reduce.11
  576.1 116.6 reduce-scatter.3
where the time goes:
time: 718 us; the launch traced here: 717 us
  waiting for transfers between devices  387 us (54%)
  blocking collectives  157 us (22%)
  other arithmetic  84.8 us (12%)
  matrix products  41.1 us (6%)
  local copies, waits for them, and re-layouts  32.2 us (4%)
  between operations  13.8 us (2%)
    psum x2, waiting for transfers between devices, per_device(): lax.psum(jnp.sum(exp_table * row_scale[:, None], axis=0), 'dp')  162 us
    pmax x1, blocking collectives, per_device(): lax.pmax(jnp.max(scores, axis=0).astype(jnp.bfloat16), 'dp')  125 us
    unnamed x6, waiting for transfers between devices  119 us
    psum x1, waiting for transfers between devices, per_device(): col_total = lax.psum(jnp.sum(exp_table, axis=0), 'dp')  97.2 us
    unnamed x7, local copies, waits for them, and re-layouts  32.2 us
    reduce_sum x3, other arithmetic, per_device(): jnp.sum(exp_table * col_scale[None, :], axis=1)  26.4 us
    psum x3, blocking collectives, per_device(): lax.psum(jnp.sum(exp_table * col_scale[None, :], axis=1), 'proto')  25.4 us
    reduce_sum x2, other arithmetic, per_device(): jnp.sum(exp_table * row_scale[:, None], axis=0)  18.5 us
  transfers between devices with their start and end apart: 5, of which 5 were waited for; matrix products, arithmetic and copies ran while one was open for 7% of the time, Pallas kernels for 0%

commit v1 on v0

v1 whole, which is shorter than its diff:
```python
import functools
import math

import jax
import jax.numpy as jnp
from jax import lax
from jax.experimental import pallas as pl
from jax.experimental.pallas import tpu as pltpu
from jax.sharding import PartitionSpec as P

MESH = pl.DeviceIdType.MESH
F32 = jnp.float32
BF16 = jnp.bfloat16

TEACHER_TEMP = 0.04
STUDENT_TEMP = 0.1
LOG2E = math.log2(math.e)
T_EXP = LOG2E / TEACHER_TEMP
S_EXP = LOG2E / STUDENT_TEMP

NX, NY, NZ, NC = 4, 4, 4, 2
BLK = 256
ROWS = NX * BLK
COLS = 4096
CH = 512
NCH = COLS // CH
D = 256
ITERS = 3


def kernel(
    tf_hbm, tp_hbm, sf_hbm, sp_hbm, outp, outf,
    E, S, G, Tp, Sp, SpT, Tf, Sf, SfT, racc, rbc, gbc, smx, sfac,
    mb, sb, cvec, col1, col1_in, col2, col2_in, rowp, row_in, stat, stat_in,
    gp, gp_in, zs, zs_in, xs, gfs, gfs_in, gfown,
    local_sem, t_send, t_recv, s_send, s_recv, c1_send, c1_recv, c_send, c_recv,
    r_send, r_recv, st_send, st_recv, gp_send, gp_recv, z_send, z_recv, x_send, x_recv,
    f_send, f_recv, y_send, y_recv,
):
    dp = lax.axis_index("dp")
    y = lax.axis_index("proto")
    z, x, c = dp // 8, (dp // 2) % 4, dp % 2

    def dev(dz, dx, dc, dy):
        zz, xx, cc, yy = (z + dz) % NZ, (x + dx) % NX, (c + dc) % NC, (y + dy) % NY
        return {"dp": zz * 8 + xx * 2 + cc, "proto": yy}

    xy = [(a, b) for a in range(NX) for b in range(NY) if (a, b) != (0, 0)]
    zc = [(a, b) for a in range(NZ) for b in range(NC) if (a, b) != (0, 0)]

    def send(src, dst, ssem, rsem, where):
        pltpu.make_async_remote_copy(
            src_ref=src, dst_ref=dst, send_sem=ssem, recv_sem=rsem, device_id=where, device_id_type=MESH
        ).start()

    def take(ref, sem):
        pltpu.make_async_copy(ref, ref, sem).wait()

    barrier = pltpu.get_barrier_semaphore()
    for a, b in xy:
        pl.semaphore_signal(barrier, inc=1, device_id=dev(0, a, 0, b), device_id_type=MESH)
    for a, b in zc:
        pl.semaphore_signal(barrier, inc=1, device_id=dev(a, 0, b, 0), device_id_type=MESH)

    mine = pl.ds(pl.multiple_of(x * COLS, COLS), COLS)
    loads = [
        pltpu.make_async_copy(tf_hbm, Tf.at[x], local_sem.at[0]),
        pltpu.make_async_copy(sf_hbm, Sf.at[x], local_sem.at[1]),
        pltpu.make_async_copy(tp_hbm.at[:, mine], Tp, local_sem.at[2]),
        pltpu.make_async_copy(sp_hbm.at[:, mine], Sp, local_sem.at[3]),
    ]
    for load in loads:
        load.start()
    loads[0].wait()
    loads[1].wait()
    pl.semaphore_wait(barrier, len(xy) + len(zc))
    for a in (1, 3, 2):
        send(Tf.at[x], Tf.at[x], t_send, t_recv.at[x], dev(0, a, 0, 0))
    for a in (1, 3, 2):
        send(Sf.at[x], Sf.at[x], s_send, s_recv.at[x], dev(0, a, 0, 0))

    def chunk(j):
        return pl.ds(pl.multiple_of(j * CH, CH), CH)

    def rows_at(i, n):
        return pl.ds(pl.multiple_of(i * n, n), n)

    def teacher_block(a):
        def body(j, _):
            s = jnp.dot(Tf[a], Tp[:, chunk(j)], preferred_element_type=F32)
            m = jnp.max(s, axis=0, keepdims=True)
            e = jnp.exp2((s - m) * T_EXP)
            E[rows_at(a, BLK), chunk(j)] = e
            mb[a, pl.ds(j, 1), :] = m
            sb[a, pl.ds(j, 1), :] = jnp.sum(e, axis=0, keepdims=True)
            return 0
        lax.fori_loop(0, NCH, body, 0)

    def lane_parts(v, op):
        out = v[:, :128]
        for q in range(1, v.shape[1] // 128):
            out = op(out, v[:, q * 128:(q + 1) * 128])
        return out

    def to_lanes(src, dst, op):
        for i in range(8):
            t = src[i * 128:(i + 1) * 128, :].T
            dst[i:i + 1, :] = op(t, axis=0, keepdims=True)

    def to_rows(v, dst):
        for i in range(8):
            dst[i * 128:(i + 1) * 128, :] = jnp.broadcast_to(v[i:i + 1, :], (128, 128)).T

    def student_block(a):
        base = a * BLK
        block = rows_at(a, BLK)

        def scores(j, _):
            s = jnp.dot(Sf[a], Sp[:, chunk(j)], preferred_element_type=F32)
            S[block, chunk(j)] = s
            m = lane_parts(s, jnp.maximum)

            @pl.when(j == 0)
            def _():
                smx[block, :] = m

            @pl.when(j > 0)
            def _():
                smx[block, :] = jnp.maximum(smx[block, :], m)
            return 0
        lax.fori_loop(0, NCH, scores, 0)

        def exps(i, _):
            r = pl.ds(pl.multiple_of(base + i * 64, 64), 64)
            m = jnp.broadcast_to(jnp.max(smx[r, :], axis=1, keepdims=True), (64, 128))
            smx[r, :] = m
            acc = jnp.zeros((64, 128), F32)
            for q in range(COLS // 128):
                e = jnp.exp2((S[r, q * 128:(q + 1) * 128] - m) * S_EXP)
                S[r, q * 128:(q + 1) * 128] = e
                acc = acc + e
            sfac[r, :] = acc
            return 0
        lax.fori_loop(0, BLK // 64, exps, 0)

    def row_pass(first, last):
        def body(i, _):
            r = rows_at(i, 64)
            acc = jnp.zeros((64, 128), F32)
            for j in range(NCH):
                for q in range(CH // 128):
                    at = j * CH + q * 128
                    e = E[r, at:at + 128]
                    if first:
                        e = e * col1[0, j:j + 1, q * 128:(q + 1) * 128]
                        E[r, at:at + 128] = e
                    e = e * cvec[j:j + 1, q * 128:(q + 1) * 128]
                    if last:
                        E[r, at:at + 128] = e
                    acc = acc + e
            racc[r, :] = acc
            return 0
        if first:
            for a in range(NX):
                col1[0] = mb[a]
                lax.fori_loop(a * BLK // 64, (a + 1) * BLK // 64, body, 0)
        else:
            lax.fori_loop(0, ROWS // 64, body, 0)

    def row_start(t):
        to_lanes(racc, rowp.at[t], jnp.sum)
        for n, (a, b) in enumerate(xy):
            send(rowp.at[t], row_in.at[t, n], r_send.at[t], r_recv.at[t], dev(0, a, 0, b))

    def row_end(t):
        take(row_in.at[t], r_recv.at[t])
        total = rowp[t]
        for n in range(len(xy)):
            total = total + row_in[t, n]
        return 1.0 / total

    def col_pass():
        half = COLS // 2
        for h in range(2):
            def body(i, acc):
                r = rows_at(i, 64)
                rb = rbc[r, :]
                parts = []
                for q in range(half // 128):
                    p = E[r, h * half + q * 128:h * half + (q + 1) * 128] * rb
                    parts.append(acc[q] + jnp.sum(p.reshape(8, 8, 128), axis=0))
                return tuple(parts)
            acc = lax.fori_loop(
                0, ROWS // 64, body, tuple(jnp.zeros((8, 128), F32) for _ in range(half // 128))
            )
            for q in range(half // 128):
                k = h * half + q * 128
                yield k, jnp.sum(acc[q], axis=0, keepdims=True)

    def col_start(t):
        for k, v in col_pass():
            col2[t, k // CH:k // CH + 1, k % CH:k % CH + 128] = v
        for n, (a, b) in enumerate(zc):
            send(col2.at[t], col2_in.at[t, n], c_send.at[t], c_recv.at[t], dev(a, 0, b, 0))

    def col_end(t):
        take(col2_in.at[t], c_recv.at[t])
        total = col2[t]
        for n in range(len(zc)):
            total = total + col2_in[t, n]
        cvec[...] = 1.0 / total

    loads[2].wait()
    teacher_block(x)
    loads[3].wait()
    student_block(x)
    for a in (1, 3, 2):
        other = (x + a) % NX
        take(Tf.at[other], t_recv.at[other])
        teacher_block(other)

    m_loc = jnp.maximum(jnp.maximum(mb[0], mb[1]), jnp.maximum(mb[2], mb[3]))
    tot = jnp.zeros((NCH, CH), F32)
    for a in range(NX):
        tot = tot + sb[a] * jnp.exp2((mb[a] - m_loc) * T_EXP)
    col1[0] = m_loc
    col1[1] = tot
    for n, (a, b) in enumerate(zc):
        send(col1, col1_in.at[n], c1_send, c1_recv, dev(a, 0, b, 0))

    for a in (1, 3):
        other = (x + a) % NX
        take(Sf.at[other], s_recv.at[other])
        student_block(other)

    take(col1_in, c1_recv)
    for n in range(len(zc)):
        take(col1, c1_send)
    top = col1[0]
    for n in range(len(zc)):
        top = jnp.maximum(top, col1_in[n, 0])
    tot = col1[1] * jnp.exp2((col1[0] - top) * T_EXP)
    for n in range(len(zc)):
        tot = tot + col1_in[n, 1] * jnp.exp2((col1_in[n, 0] - top) * T_EXP)
    cvec[...] = 1.0 / tot
    for a in range(NX):
        mb[a] = jnp.exp2((mb[a] - top) * T_EXP)

    row_pass(True, False)
    row_start(0)
    other = (x + 2) % NX
    take(Sf.at[other], s_recv.at[other])
    student_block(other)
    to_lanes(smx, stat.at[0], jnp.max)
    to_lanes(sfac, stat.at[1], jnp.sum)
    for n, (a, b) in enumerate(xy):
        send(stat, stat_in.at[n], st_send, st_recv, dev(0, a, 0, b))
    to_rows(row_end(0), rbc)

    col_start(0)
    for a in range(NX):
        SfT[:, a * BLK:(a + 1) * BLK] = Sf[a].T

    def flip(i, _):
        k = pl.ds(pl.multiple_of(i * D, D), D)
        SpT[k, :] = Sp[:, k].T
        return 0
    lax.fori_loop(0, COLS // D, flip, 0)
    col_end(0)

    row_pass(False, False)
    row_start(1)
    take(stat_in, st_recv)
    top = stat[0]
    for n in range(len(xy)):
        top = jnp.maximum(top, stat_in[n, 0])
    tot = stat[1] * jnp.exp2((stat[0] - top) * S_EXP)
    for n in range(len(xy)):
        tot = tot + stat_in[n, 1] * jnp.exp2((stat_in[n, 0] - top) * S_EXP)
    gain = 16 * COLS / STUDENT_TEMP
    to_rows(jnp.exp2((stat[0] - top) * S_EXP) / tot * gain, gbc)

    def scale_student(i, _):
        r = rows_at(i, 64)
        g = gbc[r, :]
        for q in range(COLS // 128):
            S[r, q * 128:(q + 1) * 128] = S[r, q * 128:(q + 1) * 128] * g
        return 0
    lax.fori_loop(0, ROWS // 64, scale_student, 0)
    to_rows(row_end(1), rbc)

    col_start(1)
    col_end(1)
    row_pass(False, True)
    row_start(2)
    to_rows(row_end(2) * gain, rbc)

    def stage_g(j):
        def body(i, _):
            r = rows_at(i, 64)
            rb = rbc[r, :]
            for q in range(CH // 128):
                k = pl.ds(pl.multiple_of(j * CH + q * 128, 128), 128)
                G[r, k] = (S[r, k] - E[r, k] * rb).astype(BF16)
            return 0
        lax.fori_loop(0, ROWS // 64, body, 0)
        part = jnp.dot(SfT[...], G[:, chunk(j)], preferred_element_type=F32)
        gp[j] = part.reshape(16, NC, 8, CH)
        send(gp.at[j, :, 1 - c], gp_in.at[j], gp_send, gp_recv.at[j], dev(0, 0, 1, 0))

    def stage_c(j):
        take(gp_in.at[j], gp_recv.at[j])
        both = gp[j, :, c] + gp_in[j]
        gp_in[j] = both
        zs[j] = both.reshape(NZ, 4 * 8, CH).astype(BF16)
        for a in (1, 3, 2):
            send(zs.at[j, (z + a) % NZ], zs_in.at[j, a - 1], z_send, z_recv.at[j], dev(a, 0, 0, 0))

    def stage_z(j):
        take(zs_in.at[j], z_recv.at[j])
        total = gp_in[j, pl.ds(z * 4, 4)]
        for a in range(3):
            total = total + zs_in[j, a].astype(F32).reshape(NX, 8, CH)
        xs[j] = total * (1.0 / math.sqrt(BLK * 32))
        here = pl.ds(pl.multiple_of(x * COLS + j * CH, CH), CH)
        outp[:, here] = xs[j, x]
        for a in (1, 3, 2):
            send(xs.at[j, (x + a) % NX], outp.at[:, here], x_send, x_recv, dev(0, a, 0, 0))

    def stage_f(a):
        block = (x + a) % NX
        part = jnp.dot(G[rows_at(block, BLK), :], SpT[...], preferred_element_type=F32)
        gfs[block] = part.astype(BF16)
        if a == 0:
            gfown[...] = part
        for b in range(NY):
            if a or b:
                quarter = pl.ds(pl.multiple_of((y + b) % NY * 64, 64), 64)
                send(gfs.at[block, quarter], gfs_in.at[a * 4 + b - 1], f_send, f_recv, dev(0, a, 0, b))

    stage_g(0)
    stage_g(1)
    stage_c(0)

    def steady(j, _):
        stage_g(j)
        stage_c(j - 1)
        stage_z(j - 2)
        return 0
    lax.fori_loop(2, NCH, steady, 0)
    stage_f(2)
    stage_c(NCH - 1)
    stage_f(1)
    stage_f(3)
    stage_z(NCH - 2)
    stage_f(0)
    stage_z(NCH - 1)

    take(gfs_in, f_recv)
    own = pl.ds(pl.multiple_of(y * 64, 64), 64)
    total = gfown[own, :]
    for n in range(len(xy)):
        total = total + gfs_in[n].astype(F32)
    outf[own, :] = total * (1.0 / math.sqrt(16 * COLS))
    for b in (1, 3, 2):
        send(outf.at[own, :], outf.at[own, :], y_send, y_recv, dev(0, 0, 0, b))
    take(outp.at[:, pl.ds(0, 3 * COLS)], x_recv)
    take(outf.at[pl.ds(0, 192), :], y_recv)

    for n in range(3):
        take(Tf.at[0], t_send)
        take(Sf.at[0], s_send)
    for t in range(ITERS):
        take(row_in.at[t], r_send.at[t])
    for t in range(ITERS - 1):
        take(col2_in.at[t], c_send.at[t])
    take(stat_in, st_send)
    take(gp_in, gp_send)
    take(zs_in, z_send)
    take(outp.at[:, pl.ds(0, 3 * COLS)], x_send)
    take(gfs_in, f_send)
    take(outf.at[pl.ds(0, 192), :], y_send)


def per_device(teacher_feats, teacher_protos, student_feats, student_protos):
    V, sem = pltpu.VMEM, pltpu.SemaphoreType.DMA
    scratch = [
        V((ROWS, COLS), F32), V((ROWS, COLS), F32), V((ROWS, COLS), BF16),
        V((D, COLS), BF16), V((D, COLS), BF16), V((COLS, D), BF16),
        V((NX, BLK, D), BF16), V((NX, BLK, D), BF16), V((D, ROWS), BF16),
        V((ROWS, 128), F32), V((ROWS, 128), F32), V((ROWS, 128), F32), V((ROWS, 128), F32), V((ROWS, 128), F32),
        V((NX, NCH, CH), F32), V((NX, NCH, CH), F32), V((NCH, CH), F32),
        V((2, NCH, CH), F32), V((7, 2, NCH, CH), F32), V((2, NCH, CH), F32), V((2, 7, NCH, CH), F32),
        V((ITERS, 8, 128), F32), V((ITERS, 15, 8, 128), F32), V((2, 8, 128), F32), V((15, 2, 8, 128), F32),
        V((NCH, 16, NC, 8, CH), F32), V((NCH, 16, 8, CH), F32),
        V((NCH, NZ, 32, CH), BF16), V((NCH, 3, 32, CH), BF16), V((NCH, NX, 8, CH), F32),
        V((NX, BLK, D), BF16), V((15, 64, D), BF16), V((BLK, D), F32),
        sem((4,)), sem, sem((NX,)), sem, sem((NX,)), sem, sem, sem((2,)), sem((2,)),
        sem((ITERS,)), sem((ITERS,)), sem, sem, sem, sem((NCH,)), sem, sem((NCH,)), sem, sem,
        sem, sem, sem, sem,
    ]
    any_spec = pl.BlockSpec(memory_space=pl.ANY)
    vmem_spec = pl.BlockSpec(memory_space=pltpu.VMEM)
    return pl.pallas_call(
        kernel,
        out_shape=(
            jax.ShapeDtypeStruct((8, NX * COLS), F32),
            jax.ShapeDtypeStruct((BLK, D), F32),
        ),
        in_specs=[any_spec] * 4,
        out_specs=(vmem_spec, vmem_spec),
        scratch_shapes=scratch,
        compiler_params=pltpu.CompilerParams(
            collective_id=0, has_side_effects=True, vmem_limit_bytes=62 << 20
        ),
    )(teacher_feats, teacher_protos, student_feats, student_protos)


def solution(mesh):
    return jax.shard_map(
        per_device,
        mesh=mesh,
        in_specs=(P("dp", None), P(None, "proto"), P("dp", None), P(None, "proto")),
        out_specs=(P("dp", "proto"), P("dp", None)),
        check_vma=False,
    )
```

time: 718 us -> 104 us (0.14)
  waiting for transfers between devices: 387 us -> 0 us
  blocking collectives: 157 us -> 0 us
  Pallas kernels: 0 us -> 99.5 us
  other arithmetic: 84.8 us -> 0 us
  matrix products: 41.1 us -> 0 us
  local copies, waits for them, and re-layouts: 32.2 us -> 3.54 us
  between operations: 13.8 us -> 0.64 us
    psum x4 -> x0, waiting for transfers between devices: 268 us -> none  [the longest x2 162 us: per_device(): lax.psum(jnp.sum(exp_table * row_scale[:, None], axis=0), 'dp')]
    pmax x2 -> x0, blocking collectives: 131 us -> none  [the longest x1 125 us: per_device(): lax.pmax(jnp.max(scores, axis=0).astype(jnp.bfloat16), 'dp')]
    unnamed x6 -> x0, waiting for transfers between devices: 119 us -> none
    pallas_call x0 -> x1, Pallas kernels: none -> 99.5 us  [per_device(): pl.pallas_call(kernel, out_shape=(jax.ShapeDtypeStruct((8, NX * COLS), F3...]
    reduce_sum x7 -> x0, other arithmetic: 62 us -> none  [the longest x3 26.4 us: per_device(): jnp.sum(exp_table * col_scale[None, :], axis=1)]
    dot_general x4 -> x0, matrix products: 41.1 us -> none  [the longest x1 11.6 us: per_device(): jnp.dot(teacher_feats, teacher_protos, preferred_element_type=jnp.float32)]
    unnamed x7 -> x2, local copies, waits for them, and re-layouts: 32.2 us -> 3.54 us
    psum x3 -> x0, blocking collectives: 25.4 us -> none  [per_device(): lax.psum(jnp.sum(exp_table * col_scale[None, :], axis=1), 'proto')]
  transfers between devices with their start and end apart: 5 -> 0, of which waited for: 5 -> 0; matrix products, arithmetic and copies ran while one was open for 7% -> 0% of each run, Pallas kernels for 0% -> 0%
where the time goes in v1:
time: 104 us
  Pallas kernels  99.5 us (96%)
  local copies, waits for them, and re-layouts  3.54 us (3%)
    pallas_call x1, Pallas kernels, per_device(): pl.pallas_call(kernel, out_shape=(jax.ShapeDtypeStruct((8, NX * COLS), F3...  99.5 us
    unnamed x2, local copies, waits for them, and re-layouts  3.54 us

profile of v1, /device:TPU:1, one launch (start us, length us, event | category | flops | bytes accessed | tf_op | source)
XLA Modules:
  0.0 103.7 jit_solution(15710366094239454874)
XLA Ops:
  0.6 99.5 %shard_map.59 = (f32[8,16384]{1,0:T(8,128)}, f32[256,256]{1,0:T(8,128)}) custom-call(bf16[256,256]{1,0:T(8,128)(2,1)} %tf_hbm.1, bf16[256,16384]{1,0:T(8,128)(2,1)} %tp_hbm.1, bf16[256,256]{1,0:T(8,128)(2,1)} %sf_hbm.1, bf16[256,16384]{1,0:T(8,128)(2,1)} %sp_hbm.1), custom_call_target="tpu_custom_call" | custom-call | tf_op jit(solution)/shard_map/pallas_call | solution.py:404
  100.1 1.9 %copy.8 = f32[8,16384]{1,0:T(8,128)} copy(f32[8,16384]{1,0:T(8,128)} %get-tuple-element.4) | data formatting | bytes 1048576
  102.0 1.7 %copy.9 = f32[256,256]{1,0:T(8,128)} copy(f32[256,256]{1,0:T(8,128)} %get-tuple-element.5) | data formatting | bytes 524288

commit v2 on v1

--- a/solution.py
+++ b/solution.py
@@ -25,6 +25,7 @@
 CH = 512
 NCH = COLS // CH
 D = 256
+GP = 4
 ITERS = 3
 
 
@@ -56,6 +57,12 @@
     def take(ref, sem):
         pltpu.make_async_copy(ref, ref, sem).wait()
 
+    def chunk(j):
+        return pl.ds(pl.multiple_of(j * CH, CH), CH)
+
+    def rows_at(i, n):
+        return pl.ds(pl.multiple_of(i * n, n), n)
+
     barrier = pltpu.get_barrier_semaphore()
     for a, b in xy:
         pl.semaphore_signal(barrier, inc=1, device_id=dev(0, a, 0, b), device_id_type=MESH)
@@ -65,36 +72,26 @@
     mine = pl.ds(pl.multiple_of(x * COLS, COLS), COLS)
     loads = [
         pltpu.make_async_copy(tf_hbm, Tf.at[x], local_sem.at[0]),
-        pltpu.make_async_copy(sf_hbm, Sf.at[x], local_sem.at[1]),
+        pltpu.make_async_copy(sf_hbm, Sf.at[rows_at(x, BLK)], local_sem.at[1]),
         pltpu.make_async_copy(tp_hbm.at[:, mine], Tp, local_sem.at[2]),
         pltpu.make_async_copy(sp_hbm.at[:, mine], Sp, local_sem.at[3]),
     ]
     for load in loads:
         load.start()
-    loads[0].wait()
-    loads[1].wait()
     pl.semaphore_wait(barrier, len(xy) + len(zc))
     for a in (1, 3, 2):
-        send(Tf.at[x], Tf.at[x], t_send, t_recv.at[x], dev(0, a, 0, 0))
-    for a in (1, 3, 2):
-        send(Sf.at[x], Sf.at[x], s_send, s_recv.at[x], dev(0, a, 0, 0))
-
-    def chunk(j):
-        return pl.ds(pl.multiple_of(j * CH, CH), CH)
-
-    def rows_at(i, n):
-        return pl.ds(pl.multiple_of(i * n, n), n)
+        send(tf_hbm, Tf.at[x], t_send, t_recv.at[x], dev(0, a, 0, 0))
 
     def teacher_block(a):
-        def body(j, _):
-            s = jnp.dot(Tf[a], Tp[:, chunk(j)], preferred_element_type=F32)
+        block = rows_at(a, BLK)
+        for j in range(NCH):
+            k = slice(j * CH, (j + 1) * CH)
+            s = jnp.dot(Tf[a], Tp[:, k], preferred_element_type=F32)
             m = jnp.max(s, axis=0, keepdims=True)
             e = jnp.exp2((s - m) * T_EXP)
-            E[rows_at(a, BLK), chunk(j)] = e
-            mb[a, pl.ds(j, 1), :] = m
-            sb[a, pl.ds(j, 1), :] = jnp.sum(e, axis=0, keepdims=True)
-            return 0
-        lax.fori_loop(0, NCH, body, 0)
+            E[block, k] = e
+            mb[a, j:j + 1, :] = m
+            sb[a, j:j + 1, :] = jnp.sum(e, axis=0, keepdims=True)
 
     def lane_parts(v, op):
         out = v[:, :128]
@@ -111,29 +108,22 @@
         for i in range(8):
             dst[i * 128:(i + 1) * 128, :] = jnp.broadcast_to(v[i:i + 1, :], (128, 128)).T
 
-    def student_block(a):
-        base = a * BLK
-        block = rows_at(a, BLK)
-
-        def scores(j, _):
-            s = jnp.dot(Sf[a], Sp[:, chunk(j)], preferred_element_type=F32)
-            S[block, chunk(j)] = s
+    def student_scores():
+        for j in range(NCH):
+            k = slice(j * CH, (j + 1) * CH)
+            s = jnp.dot(Sf[...], Sp[:, k], preferred_element_type=F32)
+            S[:, k] = s
             m = lane_parts(s, jnp.maximum)
-
-            @pl.when(j == 0)
-            def _():
-                smx[block, :] = m
-
-            @pl.when(j > 0)
-            def _():
-                smx[block, :] = jnp.maximum(smx[block, :], m)
-            return 0
-        lax.fori_loop(0, NCH, scores, 0)
-
-        def exps(i, _):
-            r = pl.ds(pl.multiple_of(base + i * 64, 64), 64)
-            m = jnp.broadcast_to(jnp.max(smx[r, :], axis=1, keepdims=True), (64, 128))
-            smx[r, :] = m
+            smx[...] = m if j == 0 else jnp.maximum(smx[...], m)
+
+    def student_exps():
+        for i in range(ROWS // 128):
+            r = slice(i * 128, (i + 1) * 128)
+            smx[r, :] = jnp.broadcast_to(jnp.max(smx[r, :], axis=1, keepdims=True), (128, 128))
+
+        def body(i, _):
+            r = rows_at(i, 64)
+            m = smx[r, :]
             acc = jnp.zeros((64, 128), F32)
             for q in range(COLS // 128):
                 e = jnp.exp2((S[r, q * 128:(q + 1) * 128] - m) * S_EXP)
@@ -141,7 +131,7 @@
                 acc = acc + e
             sfac[r, :] = acc
             return 0
-        lax.fori_loop(0, BLK // 64, exps, 0)
+        lax.fori_loop(0, ROWS // 64, body, 0)
 
     def row_pass(first, last):
         def body(i, _):
@@ -152,7 +142,7 @@
                     at = j * CH + q * 128
                     e = E[r, at:at + 128]
                     if first:
-                        e = e * col1[0, j:j + 1, q * 128:(q + 1) * 128]
+                        e = e * col1[j:j + 1, q * 128:(q + 1) * 128]
                         E[r, at:at + 128] = e
                     e = e * cvec[j:j + 1, q * 128:(q + 1) * 128]
                     if last:
@@ -162,7 +152,7 @@
             return 0
         if first:
             for a in range(NX):
-                col1[0] = mb[a]
+                col1[...] = mb[a]
                 lax.fori_loop(a * BLK // 64, (a + 1) * BLK // 64, body, 0)
         else:
             lax.fori_loop(0, ROWS // 64, body, 0)
@@ -210,66 +200,70 @@
             total = total + col2_in[t, n]
         cvec[...] = 1.0 / total
 
+    loads[0].wait()
     loads[2].wait()
     teacher_block(x)
-    loads[3].wait()
-    student_block(x)
+    loads[1].wait()
     for a in (1, 3, 2):
         other = (x + a) % NX
         take(Tf.at[other], t_recv.at[other])
+        if a == 3:
+            for d in (1, 3, 2):
+                send(sf_hbm, Sf.at[rows_at(x, BLK)], s_send, s_recv.at[x], dev(0, d, 0, 0))
         teacher_block(other)
 
     m_loc = jnp.maximum(jnp.maximum(mb[0], mb[1]), jnp.maximum(mb[2], mb[3]))
     tot = jnp.zeros((NCH, CH), F32)
     for a in range(NX):
         tot = tot + sb[a] * jnp.exp2((mb[a] - m_loc) * T_EXP)
-    col1[0] = m_loc
-    col1[1] = tot
+    col1[...] = m_loc + jnp.log(tot) * TEACHER_TEMP
     for n, (a, b) in enumerate(zc):
         send(col1, col1_in.at[n], c1_send, c1_recv, dev(a, 0, b, 0))
 
-    for a in (1, 3):
-        other = (x + a) % NX
-        take(Sf.at[other], s_recv.at[other])
-        student_block(other)
-
-    take(col1_in, c1_recv)
-    for n in range(len(zc)):
-        take(col1, c1_send)
-    top = col1[0]
-    for n in range(len(zc)):
-        top = jnp.maximum(top, col1_in[n, 0])
-    tot = col1[1] * jnp.exp2((col1[0] - top) * T_EXP)
-    for n in range(len(zc)):
-        tot = tot + col1_in[n, 1] * jnp.exp2((col1_in[n, 0] - top) * T_EXP)
-    cvec[...] = 1.0 / tot
-    for a in range(NX):
-        mb[a] = jnp.exp2((mb[a] - top) * T_EXP)
-
-    row_pass(True, False)
-    row_start(0)
-    other = (x + 2) % NX
-    take(Sf.at[other], s_recv.at[other])
-    student_block(other)
-    to_lanes(smx, stat.at[0], jnp.max)
-    to_lanes(sfac, stat.at[1], jnp.sum)
-    for n, (a, b) in enumerate(xy):
-        send(stat, stat_in.at[n], st_send, st_recv, dev(0, a, 0, b))
-    to_rows(row_end(0), rbc)
-
-    col_start(0)
-    for a in range(NX):
-        SfT[:, a * BLK:(a + 1) * BLK] = Sf[a].T
+    loads[3].wait()
 
     def flip(i, _):
         k = pl.ds(pl.multiple_of(i * D, D), D)
         SpT[k, :] = Sp[:, k].T
         return 0
     lax.fori_loop(0, COLS // D, flip, 0)
+
+    take(col1_in, c1_recv)
+    for n in range(len(zc)):
+        take(col1, c1_send)
+    top = col1[...]
+    for n in range(len(zc)):
+        top = jnp.maximum(top, col1_in[n])
+    tot = jnp.exp2((col1[...] - top) * T_EXP)
+    for n in range(len(zc)):
+        tot = tot + jnp.exp2((col1_in[n] - top) * T_EXP)
+    cvec[...] = 1.0 / tot
+    for a in range(NX):
+        mb[a] = jnp.exp2((mb[a] - top) * T_EXP)
+
+    row_pass(True, False)
+    row_start(0)
+    for a in (1, 3, 2):
+        other = (x + a) % NX
+        take(Sf.at[rows_at(other, BLK)], s_recv.at[other])
+    student_scores()
+    to_rows(row_end(0), rbc)
+
+    col_start(0)
+    student_exps()
+    to_lanes(smx, stat.at[0], jnp.max)
+    to_lanes(sfac, stat.at[1], jnp.sum)
+    for n, (a, b) in enumerate(xy):
+        send(stat, stat_in.at[n], st_send, st_recv, dev(0, a, 0, b))
     col_end(0)
 
     row_pass(False, False)
     row_start(1)
+    for a in range(NX):
+        SfT[:, a * BLK:(a + 1) * BLK] = Sf[a * BLK:(a + 1) * BLK, :].T
+    to_rows(row_end(1), rbc)
+
+    col_start(1)
     take(stat_in, st_recv)
     top = stat[0]
     for n in range(len(xy)):
@@ -287,30 +281,32 @@
             S[r, q * 128:(q + 1) * 128] = S[r, q * 128:(q + 1) * 128] * g
         return 0
     lax.fori_loop(0, ROWS // 64, scale_student, 0)
-    to_rows(row_end(1), rbc)
-
-    col_start(1)
     col_end(1)
     row_pass(False, True)
     row_start(2)
     to_rows(row_end(2) * gain, rbc)
 
-    def stage_g(j):
+    def logits(part):
         def body(i, _):
             r = rows_at(i, 64)
             rb = rbc[r, :]
-            for q in range(CH // 128):
-                k = pl.ds(pl.multiple_of(j * CH + q * 128, 128), 128)
+            for q in range(part * 8, part * 8 + 8):
+                k = slice(q * 128, (q + 1) * 128)
                 G[r, k] = (S[r, k] - E[r, k] * rb).astype(BF16)
             return 0
         lax.fori_loop(0, ROWS // 64, body, 0)
-        part = jnp.dot(SfT[...], G[:, chunk(j)], preferred_element_type=F32)
-        gp[j] = part.reshape(16, NC, 8, CH)
-        send(gp.at[j, :, 1 - c], gp_in.at[j], gp_send, gp_recv.at[j], dev(0, 0, 1, 0))
+
+    def stage_g(j):
+        slot = j % GP
+        if j >= GP:
+            take(gp_in.at[slot], gp_send.at[slot])
+        part = jnp.dot(SfT[...], G[:, j * CH:(j + 1) * CH], preferred_element_type=F32)
+        gp[slot] = part.reshape(16, NC, 8, CH)
+        send(gp.at[slot, :, 1 - c], gp_in.at[j], gp_send.at[slot], gp_recv.at[j], dev(0, 0, 1, 0))
 
     def stage_c(j):
         take(gp_in.at[j], gp_recv.at[j])
-        both = gp[j, :, c] + gp_in[j]
+        both = gp[j % GP, :, c] + gp_in[j]
         gp_in[j] = both
         zs[j] = both.reshape(NZ, 4 * 8, CH).astype(BF16)
         for a in (1, 3, 2):
@@ -338,23 +334,22 @@
                 quarter = pl.ds(pl.multiple_of((y + b) % NY * 64, 64), 64)
                 send(gfs.at[block, quarter], gfs_in.at[a * 4 + b - 1], f_send, f_recv, dev(0, a, 0, b))
 
-    stage_g(0)
-    stage_g(1)
-    stage_c(0)
-
-    def steady(j, _):
-        stage_g(j)
-        stage_c(j - 1)
-        stage_z(j - 2)
-        return 0
-    lax.fori_loop(2, NCH, steady, 0)
+    for part in range(NCH // 2):
+        logits(part)
+        for j in (2 * part, 2 * part + 1):
+            stage_g(j)
+            if j >= 2:
+                stage_c(j - 2)
+    stage_c(NCH - 2)
     stage_f(2)
     stage_c(NCH - 1)
+    stage_z(0)
     stage_f(1)
+    stage_z(1)
     stage_f(3)
-    stage_z(NCH - 2)
     stage_f(0)
-    stage_z(NCH - 1)
+    for j in range(2, 5):
+        stage_z(j)
 
     take(gfs_in, f_recv)
     own = pl.ds(pl.multiple_of(y * 64, 64), 64)
@@ -364,22 +359,36 @@
     outf[own, :] = total * (1.0 / math.sqrt(16 * COLS))
     for b in (1, 3, 2):
         send(outf.at[own, :], outf.at[own, :], y_send, y_recv, dev(0, 0, 0, b))
+    for j in range(5, NCH):
+        stage_z(j)
     take(outp.at[:, pl.ds(0, 3 * COLS)], x_recv)
     take(outf.at[pl.ds(0, 192), :], y_recv)
 
     for n in range(3):
         take(Tf.at[0], t_send)
-        take(Sf.at[0], s_send)
+        take(Sf.at[rows_at(0, BLK)], s_send)
     for t in range(ITERS):
         take(row_in.at[t], r_send.at[t])
     for t in range(ITERS - 1):
         take(col2_in.at[t], c_send.at[t])
     take(stat_in, st_send)
-    take(gp_in, gp_send)
+    for slot in range(GP):
+        take(gp_in.at[slot], gp_send.at[slot])
     take(zs_in, z_send)
     take(outp.at[:, pl.ds(0, 3 * COLS)], x_send)
     take(gfs_in, f_send)
     take(outf.at[pl.ds(0, 192), :], y_send)
+
+
+def deliver(outp, outf, outp_hbm, outf_hbm, sems):
+    copies = [
+        pltpu.make_async_copy(outp, outp_hbm, sems.at[0]),
+        pltpu.make_async_copy(outf, outf_hbm, sems.at[1]),
+    ]
+    for copy in copies:
+        copy.start()
+    for copy in copies:
+        copy.wait()
 
 
 def per_device(teacher_feats, teacher_protos, student_feats, student_protos):
@@ -387,25 +396,25 @@
     scratch = [
         V((ROWS, COLS), F32), V((ROWS, COLS), F32), V((ROWS, COLS), BF16),
         V((D, COLS), BF16), V((D, COLS), BF16), V((COLS, D), BF16),
-        V((NX, BLK, D), BF16), V((NX, BLK, D), BF16), V((D, ROWS), BF16),
+        V((NX, BLK, D), BF16), V((ROWS, D), BF16), V((D, ROWS), BF16),
         V((ROWS, 128), F32), V((ROWS, 128), F32), V((ROWS, 128), F32), V((ROWS, 128), F32), V((ROWS, 128), F32),
         V((NX, NCH, CH), F32), V((NX, NCH, CH), F32), V((NCH, CH), F32),
-        V((2, NCH, CH), F32), V((7, 2, NCH, CH), F32), V((2, NCH, CH), F32), V((2, 7, NCH, CH), F32),
+        V((NCH, CH), F32), V((7, NCH, CH), F32), V((2, NCH, CH), F32), V((2, 7, NCH, CH), F32),
         V((ITERS, 8, 128), F32), V((ITERS, 15, 8, 128), F32), V((2, 8, 128), F32), V((15, 2, 8, 128), F32),
-        V((NCH, 16, NC, 8, CH), F32), V((NCH, 16, 8, CH), F32),
+        V((GP, 16, NC, 8, CH), F32), V((NCH, 16, 8, CH), F32),
         V((NCH, NZ, 32, CH), BF16), V((NCH, 3, 32, CH), BF16), V((NCH, NX, 8, CH), F32),
         V((NX, BLK, D), BF16), V((15, 64, D), BF16), V((BLK, D), F32),
         sem((4,)), sem, sem((NX,)), sem, sem((NX,)), sem, sem, sem((2,)), sem((2,)),
-        sem((ITERS,)), sem((ITERS,)), sem, sem, sem, sem((NCH,)), sem, sem((NCH,)), sem, sem,
+        sem((ITERS,)), sem((ITERS,)), sem, sem, sem((GP,)), sem((NCH,)), sem, sem((NCH,)), sem, sem,
         sem, sem, sem, sem,
     ]
     any_spec = pl.BlockSpec(memory_space=pl.ANY)
     vmem_spec = pl.BlockSpec(memory_space=pltpu.VMEM)
-    return pl.pallas_call(
+    held = pl.pallas_call(
         kernel,
         out_shape=(
-            jax.ShapeDtypeStruct((8, NX * COLS), F32),
-            jax.ShapeDtypeStruct((BLK, D), F32),
+            pltpu.VMEM((8, NX * COLS), F32),
+            pltpu.VMEM((BLK, D), F32),
         ),
         in_specs=[any_spec] * 4,
         out_specs=(vmem_spec, vmem_spec),
@@ -414,6 +423,16 @@
             collective_id=0, has_side_effects=True, vmem_limit_bytes=62 << 20
         ),
     )(teacher_feats, teacher_protos, student_feats, student_protos)
+    return pl.pallas_call(
+        deliver,
+        out_shape=(
+            jax.ShapeDtypeStruct((8, NX * COLS), F32),
+            jax.ShapeDtypeStruct((BLK, D), F32),
+        ),
+        in_specs=[vmem_spec] * 2,
+        out_specs=(any_spec, any_spec),
+        scratch_shapes=[sem((2,))],
+    )(*(pltpu.with_memory_space_constraint(part, pltpu.VMEM) for part in held))
 
 
 def solution(mesh):

time: 104 us -> 79.7 us (0.77)
  Pallas kernels: 99.5 us -> 78.8 us
  local copies, waits for them, and re-layouts: 3.54 us -> 0 us
    pallas_call x1 -> x2, Pallas kernels: 99.5 us -> 78.8 us  [the longest x1 77.9 us: per_device(): pl.pallas_call(kernel, out_shape=(pltpu.VMEM((8, NX * COLS), F32), pltpu....]
    unnamed x2 -> x0, local copies, waits for them, and re-layouts: 3.54 us -> none
where the time goes in v2:
time: 79.7 us; the launch traced here: 79.6 us
  Pallas kernels  78.8 us (99%)
  between operations  0.8 us (1%)
    pallas_call x1, Pallas kernels, per_device(): pl.pallas_call(kernel, out_shape=(pltpu.VMEM((8, NX * COLS), F32), pltpu....  77.9 us

profile of v2, /device:TPU:1, one launch (start us, length us, event | category | flops | bytes accessed | tf_op | source)
XLA Modules:
  0.0 79.6 jit_solution(428640409588506211)
XLA Ops:
  0.6 77.9 %shard_map.59 = (f32[8,16384]{1,0:T(8,128)S(1)}, f32[256,256]{1,0:T(8,128)S(1)}) custom-call(bf16[256,256]{1,0:T(8,128)(2,1)} %tf_hbm.1, bf16[256,16384]{1,0:T(8,128)(2,1)} %tp_hbm.1, bf16[256,256]{1,0:T(8,128)(2,1)} %sf_hbm.1, bf16[256,16384]{1,0:T(8,128)(2,1)} %sp_hbm.1), custom_call_target="tpu_custom_call" | custom-call | tf_op jit(solution)/shard_map/pallas_call | solution.py:413
  78.6 0.9 %shard_map.60 = (f32[8,16384]{1,0:T(8,128)}, f32[256,256]{1,0:T(8,128)}) custom-call(f32[8,16384]{1,0:T(8,128)S(1)} %get-tuple-element.4.outp, f32[256,256]{1,0:T(8,128)S(1)} %get-tuple-element.5.outf), custom_call_target="tpu_custom_call" | custom-call | tf_op jit(solution)/shard_map/pallas_call | solution.py:426

commit v3 on v2

--- a/solution.py
+++ b/solution.py
@@ -25,6 +25,7 @@
 CH = 512
 NCH = COLS // CH
 D = 256
+HALF, PIECE = BLK // 2, BLK // 2 // NY
 GP = 4
 ITERS = 3
 
@@ -49,6 +50,8 @@
     xy = [(a, b) for a in range(NX) for b in range(NY) if (a, b) != (0, 0)]
     zc = [(a, b) for a in range(NZ) for b in range(NC) if (a, b) != (0, 0)]
 
+    far = sorted(xy, key=lambda p: -min(p[0], NX - p[0]) - min(p[1], NY - p[1]))
+
     def send(src, dst, ssem, rsem, where):
         pltpu.make_async_remote_copy(
             src_ref=src, dst_ref=dst, send_sem=ssem, recv_sem=rsem, device_id=where, device_id_type=MESH
@@ -64,10 +67,10 @@
         return pl.ds(pl.multiple_of(i * n, n), n)
 
     barrier = pltpu.get_barrier_semaphore()
-    for a, b in xy:
-        pl.semaphore_signal(barrier, inc=1, device_id=dev(0, a, 0, b), device_id_type=MESH)
-    for a, b in zc:
-        pl.semaphore_signal(barrier, inc=1, device_id=dev(a, 0, b, 0), device_id_type=MESH)
+    lines = [(0, 2, 0, 0), (0, 0, 0, 2), (0, 1, 0, 0), (0, 3, 0, 0), (0, 0, 0, 1), (0, 0, 0, 3)]
+    lines = [(a, 0, b, 0) for a, b in reversed(zc)] + lines
+    for where in lines:
+        pl.semaphore_signal(barrier, inc=1, device_id=dev(*where), device_id_type=MESH)
 
     mine = pl.ds(pl.multiple_of(x * COLS, COLS), COLS)
     loads = [
@@ -78,7 +81,7 @@
     ]
     for load in loads:
         load.start()
-    pl.semaphore_wait(barrier, len(xy) + len(zc))
+    pl.semaphore_wait(barrier, len(lines))
     for a in (1, 3, 2):
         send(tf_hbm, Tf.at[x], t_send, t_recv.at[x], dev(0, a, 0, 0))
 
@@ -220,14 +223,6 @@
     for n, (a, b) in enumerate(zc):
         send(col1, col1_in.at[n], c1_send, c1_recv, dev(a, 0, b, 0))
 
-    loads[3].wait()
-
-    def flip(i, _):
-        k = pl.ds(pl.multiple_of(i * D, D), D)
-        SpT[k, :] = Sp[:, k].T
-        return 0
-    lax.fori_loop(0, COLS // D, flip, 0)
-
     take(col1_in, c1_recv)
     for n in range(len(zc)):
         take(col1, c1_send)
@@ -246,6 +241,7 @@
     for a in (1, 3, 2):
         other = (x + a) % NX
         take(Sf.at[rows_at(other, BLK)], s_recv.at[other])
+    loads[3].wait()
     student_scores()
     to_rows(row_end(0), rbc)
 
@@ -259,6 +255,11 @@
 
     row_pass(False, False)
     row_start(1)
+    def flip(i, _):
+        k = pl.ds(pl.multiple_of(i * D, D), D)
+        SpT[k, :] = Sp[:, k].T
+        return 0
+    lax.fori_loop(0, COLS // D, flip, 0)
     for a in range(NX):
         SfT[:, a * BLK:(a + 1) * BLK] = Sf[a * BLK:(a + 1) * BLK, :].T
     to_rows(row_end(1), rbc)
@@ -323,44 +324,58 @@
         for a in (1, 3, 2):
             send(xs.at[j, (x + a) % NX], outp.at[:, here], x_send, x_recv, dev(0, a, 0, 0))
 
-    def stage_f(a):
-        block = (x + a) % NX
-        part = jnp.dot(G[rows_at(block, BLK), :], SpT[...], preferred_element_type=F32)
-        gfs[block] = part.astype(BF16)
-        if a == 0:
-            gfown[...] = part
-        for b in range(NY):
-            if a or b:
-                quarter = pl.ds(pl.multiple_of((y + b) % NY * 64, 64), 64)
-                send(gfs.at[block, quarter], gfs_in.at[a * 4 + b - 1], f_send, f_recv, dev(0, a, 0, b))
-
-    for part in range(NCH // 2):
-        logits(part)
-        for j in (2 * part, 2 * part + 1):
-            stage_g(j)
-            if j >= 2:
-                stage_c(j - 2)
-    stage_c(NCH - 2)
-    stage_f(2)
-    stage_c(NCH - 1)
+    def stage_f(h):
+        rows = [G[b * BLK + h * HALF:b * BLK + (h + 1) * HALF, :] for b in range(NX)]
+        part = jnp.dot(jnp.concatenate(rows, axis=0), SpT[...], preferred_element_type=F32)
+        part = part.reshape(NX, HALF, D)
+        gfown[h] = part
+        gfs[h] = part.astype(BF16)
+        for n, (a, b) in enumerate(far):
+            piece = pl.ds(pl.multiple_of((y + b) % NY * PIECE, PIECE), PIECE)
+            send(gfs.at[h, (x + a) % NX, piece], gfs_in.at[h, n], f_send, f_recv.at[h], dev(0, a, 0, b))
+
+    def final_f(h):
+        take(gfs_in.at[h], f_recv.at[h])
+        total = gfown[h, x, pl.ds(pl.multiple_of(y * PIECE, PIECE), PIECE)]
+        for n in range(len(xy)):
+            total = total + gfs_in[h, n].astype(F32)
+        own = pl.ds(pl.multiple_of(h * HALF + y * PIECE, PIECE), PIECE)
+        outf[own, :] = total * (1.0 / math.sqrt(16 * COLS))
+        for b in (2, 1, 3):
+            send(outf.at[own, :], outf.at[own, :], y_send, y_recv, dev(0, 0, 0, b))
+
+    logits(0)
+    stage_g(0)
+    stage_g(1)
+    stage_c(0)
+    logits(1)
+    stage_g(2)
+    stage_c(1)
+    logits(2)
+    stage_g(3)
+    stage_c(2)
+    logits(3)
+    stage_f(0)
     stage_z(0)
+    stage_c(3)
+    stage_g(4)
+    stage_g(5)
+    stage_z(1)
+    stage_c(4)
     stage_f(1)
-    stage_z(1)
-    stage_f(3)
-    stage_f(0)
-    for j in range(2, 5):
-        stage_z(j)
-
-    take(gfs_in, f_recv)
-    own = pl.ds(pl.multiple_of(y * 64, 64), 64)
-    total = gfown[own, :]
-    for n in range(len(xy)):
-        total = total + gfs_in[n].astype(F32)
-    outf[own, :] = total * (1.0 / math.sqrt(16 * COLS))
-    for b in (1, 3, 2):
-        send(outf.at[own, :], outf.at[own, :], y_send, y_recv, dev(0, 0, 0, b))
-    for j in range(5, NCH):
-        stage_z(j)
+    stage_z(2)
+    stage_c(5)
+    stage_g(6)
+    stage_g(7)
+    stage_z(3)
+    stage_c(6)
+    final_f(0)
+    stage_z(4)
+    stage_c(7)
+    stage_z(5)
+    final_f(1)
+    stage_z(6)
+    stage_z(7)
     take(outp.at[:, pl.ds(0, 3 * COLS)], x_recv)
     take(outf.at[pl.ds(0, 192), :], y_recv)
 
@@ -403,10 +418,10 @@
         V((ITERS, 8, 128), F32), V((ITERS, 15, 8, 128), F32), V((2, 8, 128), F32), V((15, 2, 8, 128), F32),
         V((GP, 16, NC, 8, CH), F32), V((NCH, 16, 8, CH), F32),
         V((NCH, NZ, 32, CH), BF16), V((NCH, 3, 32, CH), BF16), V((NCH, NX, 8, CH), F32),
-        V((NX, BLK, D), BF16), V((15, 64, D), BF16), V((BLK, D), F32),
+        V((2, NX, HALF, D), BF16), V((2, 15, PIECE, D), BF16), V((2, NX, HALF, D), F32),
         sem((4,)), sem, sem((NX,)), sem, sem((NX,)), sem, sem, sem((2,)), sem((2,)),
         sem((ITERS,)), sem((ITERS,)), sem, sem, sem((GP,)), sem((NCH,)), sem, sem((NCH,)), sem, sem,
-        sem, sem, sem, sem,
+        sem, sem((2,)), sem, sem,
     ]
     any_spec = pl.BlockSpec(memory_space=pl.ANY)
     vmem_spec = pl.BlockSpec(memory_space=pltpu.VMEM)

time: 79.7 us -> 77.9 us (0.977)
  Pallas kernels: 78.8 us -> 76.4 us
    pallas_call x1, Pallas kernels: 77.9 us -> 75.5 us  [per_device(): pl.pallas_call(kernel, out_shape=(pltpu.VMEM((8, NX * COLS), F32), pltpu....]
where the time goes in v3:
time: 77.9 us; the launch traced here: 77.2 us
  Pallas kernels  76.4 us (98%)
  between operations  0.8 us (1%)
    pallas_call x1, Pallas kernels, per_device(): pl.pallas_call(kernel, out_shape=(pltpu.VMEM((8, NX * COLS), F32), pltpu....  75.5 us

profile of v3, /device:TPU:1, one launch (start us, length us, event | category | flops | bytes accessed | tf_op | source)
XLA Modules:
  0.0 77.2 jit_solution(2760763185985945466)
XLA Ops:
  0.6 75.5 %shard_map.59 = (f32[8,16384]{1,0:T(8,128)S(1)}, f32[256,256]{1,0:T(8,128)S(1)}) custom-call(bf16[256,256]{1,0:T(8,128)(2,1)} %tf_hbm.1, bf16[256,16384]{1,0:T(8,128)(2,1)} %tp_hbm.1, bf16[256,256]{1,0:T(8,128)(2,1)} %sf_hbm.1, bf16[256,16384]{1,0:T(8,128)(2,1)} %sp_hbm.1), custom_call_target="tpu_custom_call" | custom-call | tf_op jit(solution)/shard_map/pallas_call | solution.py:428
  76.1 0.9 %shard_map.60 = (f32[8,16384]{1,0:T(8,128)}, f32[256,256]{1,0:T(8,128)}) custom-call(f32[8,16384]{1,0:T(8,128)S(1)} %get-tuple-element.4.outp, f32[256,256]{1,0:T(8,128)S(1)} %get-tuple-element.5.outf), custom_call_target="tpu_custom_call" | custom-call | tf_op jit(solution)/shard_map/pallas_call | solution.py:441

commit v4 on v3

--- a/solution.py
+++ b/solution.py
@@ -34,7 +34,7 @@
     tf_hbm, tp_hbm, sf_hbm, sp_hbm, outp, outf,
     E, S, G, Tp, Sp, SpT, Tf, Sf, SfT, racc, rbc, gbc, smx, sfac,
     mb, sb, cvec, col1, col1_in, col2, col2_in, rowp, row_in, stat, stat_in,
-    gp, gp_in, zs, zs_in, xs, gfs, gfs_in, gfown,
+    gp, gown, gp_in, zown, zs, zs_in, xs, gfs, gfs_in, gfown,
     local_sem, t_send, t_recv, s_send, s_recv, c1_send, c1_recv, c_send, c_recv,
     r_send, r_recv, st_send, st_recv, gp_send, gp_recv, z_send, z_recv, x_send, x_recv,
     f_send, f_recv, y_send, y_recv,
@@ -47,10 +47,11 @@
         zz, xx, cc, yy = (z + dz) % NZ, (x + dx) % NX, (c + dc) % NC, (y + dy) % NY
         return {"dp": zz * 8 + xx * 2 + cc, "proto": yy}
 
-    xy = [(a, b) for a in range(NX) for b in range(NY) if (a, b) != (0, 0)]
-    zc = [(a, b) for a in range(NZ) for b in range(NC) if (a, b) != (0, 0)]
-
-    far = sorted(xy, key=lambda p: -min(p[0], NX - p[0]) - min(p[1], NY - p[1]))
+    def hops(p):
+        return -min(p[0], 4 - p[0]) - min(p[1], 4 - p[1])
+
+    xy = sorted([(a, b) for a in range(NX) for b in range(NY) if (a, b) != (0, 0)], key=hops)
+    zc = sorted([(a, b) for a in range(NZ) for b in range(NC) if (a, b) != (0, 0)], key=hops)
 
     def send(src, dst, ssem, rsem, where):
         pltpu.make_async_remote_copy(
@@ -68,7 +69,7 @@
 
     barrier = pltpu.get_barrier_semaphore()
     lines = [(0, 2, 0, 0), (0, 0, 0, 2), (0, 1, 0, 0), (0, 3, 0, 0), (0, 0, 0, 1), (0, 0, 0, 3)]
-    lines = [(a, 0, b, 0) for a, b in reversed(zc)] + lines
+    lines = [(a, 0, b, 0) for a, b in zc] + lines
     for where in lines:
         pl.semaphore_signal(barrier, inc=1, device_id=dev(*where), device_id_type=MESH)
 
@@ -119,8 +120,8 @@
             m = lane_parts(s, jnp.maximum)
             smx[...] = m if j == 0 else jnp.maximum(smx[...], m)
 
-    def student_exps():
-        for i in range(ROWS // 128):
+    def student_exps(lo, hi):
+        for i in range(lo, hi):
             r = slice(i * 128, (i + 1) * 128)
             smx[r, :] = jnp.broadcast_to(jnp.max(smx[r, :], axis=1, keepdims=True), (128, 128))
 
@@ -134,7 +135,7 @@
                 acc = acc + e
             sfac[r, :] = acc
             return 0
-        lax.fori_loop(0, ROWS // 64, body, 0)
+        lax.fori_loop(lo * 2, hi * 2, body, 0)
 
     def row_pass(first, last):
         def body(i, _):
@@ -243,10 +244,11 @@
         take(Sf.at[rows_at(other, BLK)], s_recv.at[other])
     loads[3].wait()
     student_scores()
+    student_exps(0, 4)
     to_rows(row_end(0), rbc)
 
     col_start(0)
-    student_exps()
+    student_exps(4, 8)
     to_lanes(smx, stat.at[0], jnp.max)
     to_lanes(sfac, stat.at[1], jnp.sum)
     for n, (a, b) in enumerate(xy):
@@ -302,20 +304,24 @@
         if j >= GP:
             take(gp_in.at[slot], gp_send.at[slot])
         part = jnp.dot(SfT[...], G[:, j * CH:(j + 1) * CH], preferred_element_type=F32)
-        gp[slot] = part.reshape(16, NC, 8, CH)
-        send(gp.at[slot, :, 1 - c], gp_in.at[j], gp_send.at[slot], gp_recv.at[j], dev(0, 0, 1, 0))
+        part = part.reshape(16, NC, 8, CH)
+        for h in range(NC):
+            half = part[:, h].reshape(D // NC, CH)
+            gown[slot, h] = half
+            gp[slot, h] = half.astype(BF16)
+        send(gp.at[slot, 1 - c], gp_in.at[j], gp_send.at[slot], gp_recv.at[j], dev(0, 0, 1, 0))
 
     def stage_c(j):
         take(gp_in.at[j], gp_recv.at[j])
-        both = gp[j % GP, :, c] + gp_in[j]
-        gp_in[j] = both
-        zs[j] = both.reshape(NZ, 4 * 8, CH).astype(BF16)
+        both = (gown[j % GP, c] + gp_in[j].astype(F32)).reshape(NZ, 4 * 8, CH)
+        zown[j] = both
+        zs[j] = both.astype(BF16)
         for a in (1, 3, 2):
             send(zs.at[j, (z + a) % NZ], zs_in.at[j, a - 1], z_send, z_recv.at[j], dev(a, 0, 0, 0))
 
     def stage_z(j):
         take(zs_in.at[j], z_recv.at[j])
-        total = gp_in[j, pl.ds(z * 4, 4)]
+        total = zown[j, z].reshape(NX, 8, CH)
         for a in range(3):
             total = total + zs_in[j, a].astype(F32).reshape(NX, 8, CH)
         xs[j] = total * (1.0 / math.sqrt(BLK * 32))
@@ -330,7 +336,7 @@
         part = part.reshape(NX, HALF, D)
         gfown[h] = part
         gfs[h] = part.astype(BF16)
-        for n, (a, b) in enumerate(far):
+        for n, (a, b) in enumerate(xy):
             piece = pl.ds(pl.multiple_of((y + b) % NY * PIECE, PIECE), PIECE)
             send(gfs.at[h, (x + a) % NX, piece], gfs_in.at[h, n], f_send, f_recv.at[h], dev(0, a, 0, b))
 
@@ -347,34 +353,34 @@
     logits(0)
     stage_g(0)
     stage_g(1)
+    logits(1)
     stage_c(0)
-    logits(1)
     stage_g(2)
     stage_c(1)
     logits(2)
     stage_g(3)
     stage_c(2)
     logits(3)
+    stage_g(4)
+    stage_c(3)
     stage_f(0)
     stage_z(0)
-    stage_c(3)
-    stage_g(4)
     stage_g(5)
-    stage_z(1)
     stage_c(4)
     stage_f(1)
-    stage_z(2)
+    stage_z(1)
     stage_c(5)
     stage_g(6)
     stage_g(7)
+    stage_z(2)
+    stage_c(6)
     stage_z(3)
-    stage_c(6)
+    stage_c(7)
+    stage_z(4)
     final_f(0)
-    stage_z(4)
-    stage_c(7)
     stage_z(5)
+    stage_z(6)
     final_f(1)
-    stage_z(6)
     stage_z(7)
     take(outp.at[:, pl.ds(0, 3 * COLS)], x_recv)
     take(outf.at[pl.ds(0, 192), :], y_recv)
@@ -416,7 +422,8 @@
         V((NX, NCH, CH), F32), V((NX, NCH, CH), F32), V((NCH, CH), F32),
         V((NCH, CH), F32), V((7, NCH, CH), F32), V((2, NCH, CH), F32), V((2, 7, NCH, CH), F32),
         V((ITERS, 8, 128), F32), V((ITERS, 15, 8, 128), F32), V((2, 8, 128), F32), V((15, 2, 8, 128), F32),
-        V((GP, 16, NC, 8, CH), F32), V((NCH, 16, 8, CH), F32),
+        V((GP, NC, D // NC, CH), BF16), V((GP, NC, D // NC, CH), F32), V((NCH, D // NC, CH), BF16),
+        V((NCH, NZ, 32, CH), F32),
         V((NCH, NZ, 32, CH), BF16), V((NCH, 3, 32, CH), BF16), V((NCH, NX, 8, CH), F32),
         V((2, NX, HALF, D), BF16), V((2, 15, PIECE, D), BF16), V((2, NX, HALF, D), F32),
         sem((4,)), sem, sem((NX,)), sem, sem((NX,)), sem, sem, sem((2,)), sem((2,)),

time: 77.9 us -> 75.7 us (0.972)
  Pallas kernels: 76.4 us -> 74.7 us
    pallas_call x1, Pallas kernels: 75.5 us -> 73.9 us  [per_device(): pl.pallas_call(kernel, out_shape=(pltpu.VMEM((8, NX * COLS), F32), pltpu....]
where the time goes in v4:
time: 75.7 us; the launch traced here: 75.5 us
  Pallas kernels  74.7 us (99%)
  between operations  0.8 us (1%)
    pallas_call x1, Pallas kernels, per_device(): pl.pallas_call(kernel, out_shape=(pltpu.VMEM((8, NX * COLS), F32), pltpu....  73.9 us

profile of v4, /device:TPU:1, one launch (start us, length us, event | category | flops | bytes accessed | tf_op | source)
XLA Modules:
  0.0 75.5 jit_solution(12089326892470146671)
XLA Ops:
  0.6 73.9 %shard_map.59 = (f32[8,16384]{1,0:T(8,128)S(1)}, f32[256,256]{1,0:T(8,128)S(1)}) custom-call(bf16[256,256]{1,0:T(8,128)(2,1)} %tf_hbm.1, bf16[256,16384]{1,0:T(8,128)(2,1)} %tp_hbm.1, bf16[256,256]{1,0:T(8,128)(2,1)} %sf_hbm.1, bf16[256,16384]{1,0:T(8,128)(2,1)} %sp_hbm.1), custom_call_target="tpu_custom_call" | custom-call | tf_op jit(solution)/shard_map/pallas_call | solution.py:435
  74.5 0.9 %shard_map.60 = (f32[8,16384]{1,0:T(8,128)}, f32[256,256]{1,0:T(8,128)}) custom-call(f32[8,16384]{1,0:T(8,128)S(1)} %get-tuple-element.4.outp, f32[256,256]{1,0:T(8,128)S(1)} %get-tuple-element.5.outf), custom_call_target="tpu_custom_call" | custom-call | tf_op jit(solution)/shard_map/pallas_call | solution.py:448

commit v5 on v4

--- a/solution.py
+++ b/solution.py
@@ -80,8 +80,8 @@
         pltpu.make_async_copy(tp_hbm.at[:, mine], Tp, local_sem.at[2]),
         pltpu.make_async_copy(sp_hbm.at[:, mine], Sp, local_sem.at[3]),
     ]
-    for load in loads:
-        load.start()
+    loads[0].start()
+    loads[2].start()
     pl.semaphore_wait(barrier, len(lines))
     for a in (1, 3, 2):
         send(tf_hbm, Tf.at[x], t_send, t_recv.at[x], dev(0, a, 0, 0))
@@ -207,7 +207,8 @@
     loads[0].wait()
     loads[2].wait()
     teacher_block(x)
-    loads[1].wait()
+    loads[1].start()
+    loads[3].start()
     for a in (1, 3, 2):
         other = (x + a) % NX
         take(Tf.at[other], t_recv.at[other])
@@ -242,6 +243,7 @@
     for a in (1, 3, 2):
         other = (x + a) % NX
         take(Sf.at[rows_at(other, BLK)], s_recv.at[other])
+    loads[1].wait()
     loads[3].wait()
     student_scores()
     student_exps(0, 4)
@@ -352,20 +354,20 @@
 
     logits(0)
     stage_g(0)
+    logits(1)
     stage_g(1)
-    logits(1)
     stage_c(0)
     stage_g(2)
+    logits(2)
     stage_c(1)
-    logits(2)
     stage_g(3)
+    logits(3)
     stage_c(2)
-    logits(3)
     stage_g(4)
     stage_c(3)
     stage_f(0)
+    stage_g(5)
     stage_z(0)
-    stage_g(5)
     stage_c(4)
     stage_f(1)
     stage_z(1)
@@ -373,8 +375,8 @@
     stage_g(6)
     stage_g(7)
     stage_z(2)
+    stage_z(3)
     stage_c(6)
-    stage_z(3)
     stage_c(7)
     stage_z(4)
     final_f(0)

time: 75.7 us -> 75.6 us (level)
  no operation moved by 1% of the time
where the time goes in v5:
time: 75.6 us; the launch traced here: 75.5 us
  Pallas kernels  74.7 us (99%)
  between operations  0.8 us (1%)
    pallas_call x1, Pallas kernels, per_device(): pl.pallas_call(kernel, out_shape=(pltpu.VMEM((8, NX * COLS), F32), pltpu....  73.8 us

profile of v5, /device:TPU:1, one launch (start us, length us, event | category | flops | bytes accessed | tf_op | source)
XLA Modules:
  0.0 75.5 jit_solution(2436816780692721186)
XLA Ops:
  0.6 73.8 %shard_map.59 = (f32[8,16384]{1,0:T(8,128)S(1)}, f32[256,256]{1,0:T(8,128)S(1)}) custom-call(bf16[256,256]{1,0:T(8,128)(2,1)} %tf_hbm.1, bf16[256,16384]{1,0:T(8,128)(2,1)} %tp_hbm.1, bf16[256,256]{1,0:T(8,128)(2,1)} %sf_hbm.1, bf16[256,16384]{1,0:T(8,128)(2,1)} %sp_hbm.1), custom_call_target="tpu_custom_call" | custom-call | tf_op jit(solution)/shard_map/pallas_call | solution.py:437
  74.5 0.9 %shard_map.60 = (f32[8,16384]{1,0:T(8,128)}, f32[256,256]{1,0:T(8,128)}) custom-call(f32[8,16384]{1,0:T(8,128)S(1)} %get-tuple-element.4.outp, f32[256,256]{1,0:T(8,128)S(1)} %get-tuple-element.5.outf), custom_call_target="tpu_custom_call" | custom-call | tf_op jit(solution)/shard_map/pallas_call | solution.py:450
